TPU v7x, 32 devices: a whole 2x2x4 slice. The times are simulated.
32 devices in a mesh: obs: 8 (over z, x), tile: 4 (over y, core).
Axes of the slice: x: 2, y: 2, z: 4, core: 2. Of those that a mesh axis runs over, the one named last changes fastest.
Arguments:
- jacobian: bfloat16 [2048, 65536], P(('obs', 'tile')), may hold values from -0.5 to 0.5
- obs_weight: float32 [2048], P(('obs', 'tile')), may hold values from 0.1 to 10
- block_order: int32 [512], replicated, may hold values from 0 to 511, each once
- tile_pairs: int32 [8, 64, 2], P('obs'), may hold values from 0 to 63, as said below
- tile_count: int32 [8], P('obs'), may hold values from 1 to 64, as said below
Outputs:
- hessian: float32 [512, 128, 128], P(('obs', 'tile'))
Inputs may be any that keep to these rules, and one draw needn't show every extreme that they name: `tile_pairs`: slot numbers within an owner's own 64 slots; the first tile_count[j] pairs of owner j are distinct. `tile_count`: some owner has 64 live tiles.
All inputs are finite; a program needn't handle non-finite values.
Results may differ from a plain program's by a relative error of at most 0.0015.
Values may be sent and summed in bfloat16 or wider, within the bound.
A program may use at most 256 MiB of HBM per device.

v0:
```python
import jax
import jax.numpy as jnp
from jax import lax
from jax.sharding import PartitionSpec as P

BLOCK = 128


def body(jacobian, obs_weight, block_order, tile_pairs, tile_count):
    row_count = jacobian.shape[0]
    owners = lax.axis_size("obs")
    total_blocks = block_order.shape[0]
    own_blocks = total_blocks // owners
    own_width = own_blocks * BLOCK
    blocks = jacobian.reshape(row_count, total_blocks, BLOCK)
    ordered = jnp.take(blocks, block_order, axis=1)
    root_weight = jnp.sqrt(obs_weight)[:, None, None]
    scaled = (ordered.astype(jnp.float32) * root_weight).astype(jnp.bfloat16)
    outgoing = scaled.reshape(row_count, owners, own_width)
    arrived = lax.all_to_all(outgoing, "obs", split_axis=1, concat_axis=0, tiled=True)
    columns = arrived.reshape(row_count * owners, own_width)
    pair_list = tile_pairs[0]
    live_count = tile_count[0]
    slot_total = pair_list.shape[0]
    slot_ids = jnp.arange(slot_total, dtype=jnp.int32)
    is_live = slot_ids < live_count
    per_group = min(own_blocks, 8)

    def gram_group(group_index, tiles):
        first_slot = group_index * per_group
        left_cols = lax.dynamic_slice_in_dim(columns, first_slot * BLOCK, per_group * BLOCK, 1)
        gram_part = lax.dot_general(
            left_cols, columns, (((0,), (0,)), ((), ())), preferred_element_type=jnp.float32
        )
        gram_tiles = gram_part.reshape(per_group, BLOCK, own_blocks, BLOCK).transpose(0, 2, 1, 3)
        gram_tiles = gram_tiles.reshape(per_group * own_blocks, BLOCK, BLOCK)
        relative = pair_list[:, 0] - first_slot
        inside = (relative >= 0) & (relative < per_group) & is_live
        lookup = jnp.clip(relative, 0, per_group - 1) * own_blocks + pair_list[:, 1]
        picked = jnp.take(gram_tiles, lookup, axis=0)
        return jnp.where(inside[:, None, None], picked, tiles)

    all_tiles = lax.fori_loop(
        0, own_blocks // per_group, gram_group, jnp.zeros((slot_total, BLOCK, BLOCK), jnp.float32)
    )
    hessian = lax.psum_scatter(all_tiles, "tile", scatter_dimension=0, tiled=True)
    return hessian


def solution(mesh):
    return jax.shard_map(
        body,
        mesh=mesh,
        in_specs=(
            P(("obs", "tile"), None),
            P(("obs", "tile")),
            P(),
            P("obs", None, None),
            P("obs"),
        ),
        out_specs=P(("obs", "tile"), None, None),
        check_vma=False,
    )
```

profile of v0, /device:TPU:3, one launch (start us, length us, event | category | flops | bytes accessed | tf_op | source)
XLA Modules:
  0.0 871.0 jit_solution(9356469873826885423)
XLA Ops:
  6.5 0.7 compare_select_fusion.1
  7.2 0.7 compare_and_fusion
  7.9 9.0 %copy_bitcast_fusion = bf16[64,512,128]{2,0,1:T(8,128)(2,1)} fusion(bf16[64,65536]{1,0:T(8,128)(2,1)} %param.7), kind=kLoop, calls=%fused_computation.13 | loop fusion | bytes 16777216 | tf_op jit(solution)/shard_map/reshape | solution.py:15
  16.9 23.0 %gather_fusion.1 = bf16[512,64,128]{2,1,0:T(8,128)(2,1)} fusion(bf16[64,512,128]{2,0,1:T(8,128)(2,1)} %copy_bitcast_fusion, s32[1024]{0:T(1024)S(1)} %pad_clamp_fusion.1), kind=kCustom, calls=%fused_computation.1 | custom fusion | bytes 16779264 | tf_op jit(solution)/shard_map/jit(_take)/gather | solution.py:16
  40.0 12.0 %copy.17 = bf16[64,512,128]{2,1,0:T(8,128)(2,1)} copy(bf16[64,512,128]{2,0,1:T(8,128)(2,1)} %bitcast.44) | data formatting | bytes 16777216 | tf_op jit(solution)/shard_map/jit(_take)/gather | solution.py:16
  52.0 13.3 %gather.18 = bf16[64,8,8192]{2,1,0:T(8,128)(2,1)} reshape(bf16[64,512,128]{2,1,0:T(8,128)(2,1)} %copy.17) | data formatting | bytes 16777216 | tf_op jit(solution)/shard_map/jit(_take)/gather | solution.py:16
  65.3 0.1 broadcast_in_dim.74
  65.4 0.1 copy.15
  65.5 0.1 broadcast_bitcast_fusion
  65.7 10.1 %multiply_convert_fusion = bf16[64,8,8192]{2,1,0:T(8,128)(2,1)} fusion(f32[64]{0:T(128)S(1)} %sqrt.3, bf16[64,8,8192]{2,1,0:T(8,128)(2,1)} %gather.18, pred[8,8192]{1,0:T(8,128)(4,1)S(1)} %broadcast_bitcast_fusion), kind=kLoop, calls=%fused_computation.12 | loop fusion | flops 16777216 | bytes 16843008 | tf_op jit(solution)/shard_map/convert_element_type | solution.py:18
  75.8 11.2 %copy.18 = bf16[64,8,8192]{2,0,1:T(8,128)(2,1)} copy(bf16[64,8,8192]{2,1,0:T(8,128)(2,1)} %multiply_convert_fusion) | data formatting | bytes 16777216 | tf_op jit(solution)/shard_map/convert_element_type | solution.py:18
  87.0 5.9 all-to-all-start
  92.9 182.4 %all-to-all-done = bf16[64,8,8192]{2,0,1:T(8,128)(2,1)} async-done(((bf16[64,8,8192]{2,0,1:T(8,128)(2,1)}), bf16[64,8,8192]{2,0,1:T(8,128)(2,1)}, u32[]{:S(2)}, u32[]{:S(2)}) %all-to-all-start) | async-done | bytes 8388640 | tf_op jit(solution)/shard_map/all_to_all | solution.py:20
  275.3 544.4 %while.16 = (s32[]{:T(128)}, f32[64,128,128]{2,1,0:T(8,128)}, s32[64,2]{0,1:T(2,128)S(1)}, bf16[512,8192]{1,0:T(8,128)(2,1)}, s32[]{:T(128)}, /*index=5*/s32[]{:T(128)}, s32[]{:T(128)}, s32[]{:T(128)}, s32[]{:T(128)}, s32[]{:T(128)}) while((s32[]{:T(128)}, f32[64,128,128]{2,1,0:T(8,128)}, s32[64,2]{0,1:T(2,128)S(1)}, ...), condition=%wide.region_1.2_spmd.clone, body=%wide.region_0.1_spmd.clone.sunk | while | flops 8593082368 | bytes 198186960 | solution.py:43
  275.3 17.8 %convolution_bitcast_fusion.2 = f32[128,8,64,128]{3,1,2,0:T(8,128)} fusion(bf16[512,8192]{1,0:T(8,128)(2,1)} %get-tuple-element.229, s32[]{:T(128)S(6)} %select_n.78), kind=kOutput, calls=%fused_computation.3.clone.1 | convolution fusion | flops 8589934592 | bytes 42991620 | tf_op jit(solution)/shard_map/while/body/eval_jaxpr/dot_general | solution.py:32
  293.2 17.2 %copy.24 = f32[128,8,64,128]{3,2,1,0:T(8,128)S(1)} copy(f32[128,8,64,128]{3,1,2,0:T(8,128)} %convolution_bitcast_fusion.2) | data formatting | bytes 67108864 | tf_op jit(solution)/shard_map/while
  310.4 21.5 %copy.25 = f32[8,128,64,128]{3,1,2,0:T(8,128)} copy(f32[8,128,64,128]{3,2,1,0:T(8,128)S(1)} %bitcast.42) | data formatting | bytes 67108864 | tf_op jit(solution)/shard_map/while/body/eval_jaxpr/reshape | solution.py:35
  331.9 4.9 gather_fusion
  336.9 0.7 bitcast_and_fusion.2
  337.5 4.7 select_select_fusion.2
  342.2 17.8 %convolution_bitcast_fusion.2 = f32[128,8,64,128]{3,1,2,0:T(8,128)} fusion(bf16[512,8192]{1,0:T(8,128)(2,1)} %get-tuple-element.229, s32[]{:T(128)S(6)} %select_n.78), kind=kOutput, calls=%fused_computation.3.clone.1 | convolution fusion | flops 8589934592 | bytes 42991620 | tf_op jit(solution)/shard_map/while/body/eval_jaxpr/dot_general | solution.py:32
  360.1 17.2 %copy.24 = f32[128,8,64,128]{3,2,1,0:T(8,128)S(1)} copy(f32[128,8,64,128]{3,1,2,0:T(8,128)} %convolution_bitcast_fusion.2) | data formatting | bytes 67108864 | tf_op jit(solution)/shard_map/while
  377.3 21.5 %copy.25 = f32[8,128,64,128]{3,1,2,0:T(8,128)} copy(f32[8,128,64,128]{3,2,1,0:T(8,128)S(1)} %bitcast.42) | data formatting | bytes 67108864 | tf_op jit(solution)/shard_map/while/body/eval_jaxpr/reshape | solution.py:35
  398.8 5.0 gather_fusion
  403.9 0.7 bitcast_and_fusion.2
  404.5 6.0 select_select_fusion.2
  410.5 17.8 %convolution_bitcast_fusion.2 = f32[128,8,64,128]{3,1,2,0:T(8,128)} fusion(bf16[512,8192]{1,0:T(8,128)(2,1)} %get-tuple-element.229, s32[]{:T(128)S(6)} %select_n.78), kind=kOutput, calls=%fused_computation.3.clone.1 | convolution fusion | flops 8589934592 | bytes 42991620 | tf_op jit(solution)/shard_map/while/body/eval_jaxpr/dot_general | solution.py:32
  428.4 17.2 %copy.24 = f32[128,8,64,128]{3,2,1,0:T(8,128)S(1)} copy(f32[128,8,64,128]{3,1,2,0:T(8,128)} %convolution_bitcast_fusion.2) | data formatting | bytes 67108864 | tf_op jit(solution)/shard_map/while
  445.6 21.5 %copy.25 = f32[8,128,64,128]{3,1,2,0:T(8,128)} copy(f32[8,128,64,128]{3,2,1,0:T(8,128)S(1)} %bitcast.42) | data formatting | bytes 67108864 | tf_op jit(solution)/shard_map/while/body/eval_jaxpr/reshape | solution.py:35
  467.1 5.0 gather_fusion
  472.1 0.7 bitcast_and_fusion.2
  472.7 6.0 select_select_fusion.2
  478.7 17.8 %convolution_bitcast_fusion.2 = f32[128,8,64,128]{3,1,2,0:T(8,128)} fusion(bf16[512,8192]{1,0:T(8,128)(2,1)} %get-tuple-element.229, s32[]{:T(128)S(6)} %select_n.78), kind=kOutput, calls=%fused_computation.3.clone.1 | convolution fusion | flops 8589934592 | bytes 42991620 | tf_op jit(solution)/shard_map/while/body/eval_jaxpr/dot_general | solution.py:32
  496.6 17.2 %copy.24 = f32[128,8,64,128]{3,2,1,0:T(8,128)S(1)} copy(f32[128,8,64,128]{3,1,2,0:T(8,128)} %convolution_bitcast_fusion.2) | data formatting | bytes 67108864 | tf_op jit(solution)/shard_map/while
  513.8 21.5 %copy.25 = f32[8,128,64,128]{3,1,2,0:T(8,128)} copy(f32[8,128,64,128]{3,2,1,0:T(8,128)S(1)} %bitcast.42) | data formatting | bytes 67108864 | tf_op jit(solution)/shard_map/while/body/eval_jaxpr/reshape | solution.py:35
  535.3 5.0 gather_fusion
  540.3 0.7 bitcast_and_fusion.2
  541.0 6.0 select_select_fusion.2
  547.0 17.8 %convolution_bitcast_fusion.2 = f32[128,8,64,128]{3,1,2,0:T(8,128)} fusion(bf16[512,8192]{1,0:T(8,128)(2,1)} %get-tuple-element.229, s32[]{:T(128)S(6)} %select_n.78), kind=kOutput, calls=%fused_computation.3.clone.1 | convolution fusion | flops 8589934592 | bytes 42991620 | tf_op jit(solution)/shard_map/while/body/eval_jaxpr/dot_general | solution.py:32
  564.8 17.2 %copy.24 = f32[128,8,64,128]{3,2,1,0:T(8,128)S(1)} copy(f32[128,8,64,128]{3,1,2,0:T(8,128)} %convolution_bitcast_fusion.2) | data formatting | bytes 67108864 | tf_op jit(solution)/shard_map/while
  582.0 21.5 %copy.25 = f32[8,128,64,128]{3,1,2,0:T(8,128)} copy(f32[8,128,64,128]{3,2,1,0:T(8,128)S(1)} %bitcast.42) | data formatting | bytes 67108864 | tf_op jit(solution)/shard_map/while/body/eval_jaxpr/reshape | solution.py:35
  603.5 4.9 gather_fusion
  608.5 0.7 bitcast_and_fusion.2
  609.1 6.0 select_select_fusion.2
  615.1 17.8 %convolution_bitcast_fusion.2 = f32[128,8,64,128]{3,1,2,0:T(8,128)} fusion(bf16[512,8192]{1,0:T(8,128)(2,1)} %get-tuple-element.229, s32[]{:T(128)S(6)} %select_n.78), kind=kOutput, calls=%fused_computation.3.clone.1 | convolution fusion | flops 8589934592 | bytes 42991620 | tf_op jit(solution)/shard_map/while/body/eval_jaxpr/dot_general | solution.py:32
  633.0 17.2 %copy.24 = f32[128,8,64,128]{3,2,1,0:T(8,128)S(1)} copy(f32[128,8,64,128]{3,1,2,0:T(8,128)} %convolution_bitcast_fusion.2) | data formatting | bytes 67108864 | tf_op jit(solution)/shard_map/while
  650.2 21.5 %copy.25 = f32[8,128,64,128]{3,1,2,0:T(8,128)} copy(f32[8,128,64,128]{3,2,1,0:T(8,128)S(1)} %bitcast.42) | data formatting | bytes 67108864 | tf_op jit(solution)/shard_map/while/body/eval_jaxpr/reshape | solution.py:35
  671.7 4.9 gather_fusion
  676.7 0.7 bitcast_and_fusion.2
  677.3 6.0 select_select_fusion.2
  683.3 17.8 %convolution_bitcast_fusion.2 = f32[128,8,64,128]{3,1,2,0:T(8,128)} fusion(bf16[512,8192]{1,0:T(8,128)(2,1)} %get-tuple-element.229, s32[]{:T(128)S(6)} %select_n.78), kind=kOutput, calls=%fused_computation.3.clone.1 | convolution fusion | flops 8589934592 | bytes 42991620 | tf_op jit(solution)/shard_map/while/body/eval_jaxpr/dot_general | solution.py:32
  701.2 17.2 %copy.24 = f32[128,8,64,128]{3,2,1,0:T(8,128)S(1)} copy(f32[128,8,64,128]{3,1,2,0:T(8,128)} %convolution_bitcast_fusion.2) | data formatting | bytes 67108864 | tf_op jit(solution)/shard_map/while
  718.4 21.5 %copy.25 = f32[8,128,64,128]{3,1,2,0:T(8,128)} copy(f32[8,128,64,128]{3,2,1,0:T(8,128)S(1)} %bitcast.42) | data formatting | bytes 67108864 | tf_op jit(solution)/shard_map/while/body/eval_jaxpr/reshape | solution.py:35
  739.9 4.9 gather_fusion
  744.9 0.7 bitcast_and_fusion.2
  745.5 6.0 select_select_fusion.2
  751.5 17.8 %convolution_bitcast_fusion.2 = f32[128,8,64,128]{3,1,2,0:T(8,128)} fusion(bf16[512,8192]{1,0:T(8,128)(2,1)} %get-tuple-element.229, s32[]{:T(128)S(6)} %select_n.78), kind=kOutput, calls=%fused_computation.3.clone.1 | convolution fusion | flops 8589934592 | bytes 42991620 | tf_op jit(solution)/shard_map/while/body/eval_jaxpr/dot_general | solution.py:32
  769.4 17.2 %copy.24 = f32[128,8,64,128]{3,2,1,0:T(8,128)S(1)} copy(f32[128,8,64,128]{3,1,2,0:T(8,128)} %convolution_bitcast_fusion.2) | data formatting | bytes 67108864 | tf_op jit(solution)/shard_map/while
  786.6 21.5 %copy.25 = f32[8,128,64,128]{3,1,2,0:T(8,128)} copy(f32[8,128,64,128]{3,2,1,0:T(8,128)S(1)} %bitcast.42) | data formatting | bytes 67108864 | tf_op jit(solution)/shard_map/while/body/eval_jaxpr/reshape | solution.py:35
  808.1 4.9 gather_fusion
  813.1 0.7 bitcast_and_fusion.2
  813.7 6.0 select_select_fusion.2
  819.7 0.0 reduce-scatter.2.cloned.1.call-update
  819.7 44.4 %reduce-scatter.2.cloned.1.call-done = f32[16,128,128]{2,1,0:T(8,128)} async-done(((f32[64,128,128]{2,1,0:T(8,128)}), f32[16,128,128]{2,1,0:T(8,128)}) %reduce-scatter.2.cloned.1.call-update) | async-done | bytes 1048592 | tf_op jit(solution)/shard_map/reduce_scatter | solution.py:46
  (24 shorter events, 0.2 us)
Async XLA Ops:
  52.0 13.7 %copy-start.1 = (f32[64]{0:T(128)S(1)}, f32[64]{0:T(128)}, u32[]{:S(2)}) copy-start(f32[64]{0:T(128)} %param.8) | copy-start | bytes 772
  87.0 188.3 %copy-start = (s32[1,64,2]{1,2,0:T(2,128)S(1)}, s32[1,64,2]{1,2,0:T(2,128)}, u32[]{:S(2)}) copy-start(s32[1,64,2]{1,2,0:T(2,128)} %param.10) | copy-start | bytes 1540
  87.0 188.3 %all-to-all-start = ((bf16[64,8,8192]{2,0,1:T(8,128)(2,1)}), bf16[64,8,8192]{2,0,1:T(8,128)(2,1)}, u32[]{:S(2)}, u32[]{:S(2)}) async-start(bf16[64,8,8192]{2,0,1:T(8,128)(2,1)} %copy.18), calls=%async_computation | async-start | bytes 16777216 | tf_op jit(solution)/shard_map/all_to_all | solution.py:20
  92.9 771.3 %reduce-scatter.2.cloned.1.call-start = ((), (), s32[]{:S(2)}) async-start(), calls=%async_computation.2 | async-start | bytes 5242880 | tf_op jit(solution)/shard_map/reduce_scatter | solution.py:46
Sparse Core Ops, SparseCore 0:
  819.9 44.2 reduce-scatter.1
where the time goes:
time: 875 us; the launch traced here: 871 us
  local copies, waits for them, and re-layouts  418 us (48%)
  waiting for transfers between devices  227 us (26%)
  matrix products  143 us (16%)
  other arithmetic  63.6 us (7%)
  between operations  13.4 us (2%)
    all_to_all x1, waiting for transfers between devices, body(): lax.all_to_all(outgoing, 'obs', split_axis=1, concat_axis=0, tiled=True)  182 us
    reshape x8, local copies, waits for them, and re-layouts, gram_group(): gram_part.reshape(per_group, BLOCK, own_blocks, BLOCK).transpose(0, 2, 1, 3)  172 us
    dot_general x8, matrix products, gram_group(): lax.dot_general(left_cols, columns, (((0,), (0,)), ((), ())), preferred_e...  143 us
    while x8, local copies, waits for them, and re-layouts  138 us
    gather x3, local copies, waits for them, and re-layouts, body(): ordered = jnp.take(blocks, block_order, axis=1)  48.4 us
    select_n x8, other arithmetic, gram_group(): return jnp.where(inside[:, None, None], picked, tiles)  46.7 us
    reduce_scatter x1, waiting for transfers between devices, body(): lax.psum_scatter(all_tiles, 'tile', scatter_dimension=0, tiled=True)  44.4 us
    gather x8, local copies, waits for them, and re-layouts, gram_group(): picked = jnp.take(gram_tiles, lookup, axis=0)  39.7 us
  transfers between devices with their start and end apart: 2, of which 2 were waited for; matrix products, arithmetic and copies ran while one was open for 0% of the time, Pallas kernels for 0%

commit v1 on v0

v1 whole, which is shorter than its diff:
```python
import functools
import jax
import jax.numpy as jnp
from jax import lax
from jax.experimental import pallas as pl
from jax.experimental.pallas import tpu as pltpu
from jax.sharding import Mesh, PartitionSpec as P

BLOCK = 128
PARTS = 2


def order_kernel(slots, parts, per_part, order_ref, jac_ref, weight_ref, out_ref):
    dest, part = pl.program_id(0), pl.program_id(1)
    first = (part * per_part + dest) * slots
    weight = jnp.broadcast_to(weight_ref[...], (weight_ref.shape[0], BLOCK))

    def one(slot, carry):
        start = pl.multiple_of(order_ref[first + slot] * BLOCK, BLOCK)
        piece = jac_ref[:, pl.ds(start, BLOCK)].astype(jnp.float32) * weight
        out_ref[0, 0, slot] = piece.astype(jnp.bfloat16)
        return carry

    lax.fori_loop(0, slots, one, 0, unroll=4)


def order_columns(jacobian, root_weight, block_order, parts, per_part):
    rows, width = jacobian.shape
    slots = block_order.shape[0] // (parts * per_part)
    return pl.pallas_call(
        functools.partial(order_kernel, slots, parts, per_part),
        out_shape=jax.ShapeDtypeStruct((per_part, parts, slots, rows, BLOCK), jnp.bfloat16),
        grid_spec=pltpu.PrefetchScalarGridSpec(
            num_scalar_prefetch=1,
            grid=(per_part, parts),
            in_specs=[
                pl.BlockSpec((rows, width), lambda d, p, order: (0, 0)),
                pl.BlockSpec((rows, 1), lambda d, p, order: (0, 0)),
            ],
            out_specs=pl.BlockSpec((1, 1, slots, rows, BLOCK), lambda d, p, order: (d, p, 0, 0, 0)),
        ),
        compiler_params=pltpu.CompilerParams(vmem_limit_bytes=48 << 20),
    )(block_order, jacobian, root_weight)


def tile_kernel(group, pairs_ref, count_ref, cols_ref, out_ref):
    part, step = pl.program_id(0), pl.program_id(1)
    senders, slots, rows = cols_ref.shape[0], cols_ref.shape[2], cols_ref.shape[3]

    def one(index, carry):
        tile = step * group + index

        @pl.when(tile < count_ref[part])
        def _():
            a = pairs_ref[part, 2 * tile]
            b = pairs_ref[part, 2 * tile + 1]
            left = cols_ref[:, 0, a].reshape(senders * rows, BLOCK)
            right = cols_ref[:, 0, b].reshape(senders * rows, BLOCK)
            out_ref[0, index] = lax.dot_general(
                left, right, (((0,), (0,)), ((), ())), preferred_element_type=jnp.float32
            )

        @pl.when(tile >= count_ref[part])
        def _():
            out_ref[0, index] = jnp.zeros((BLOCK, BLOCK), jnp.float32)

        return carry

    lax.fori_loop(0, group, one, 0)


def partial_tiles(columns, pairs, counts):
    senders, parts, slots, rows, _ = columns.shape
    tiles = pairs.shape[1]
    group = 16
    return pl.pallas_call(
        functools.partial(tile_kernel, group),
        out_shape=jax.ShapeDtypeStruct((parts, tiles, BLOCK, BLOCK), jnp.float32),
        grid_spec=pltpu.PrefetchScalarGridSpec(
            num_scalar_prefetch=2,
            grid=(parts, tiles // group),
            in_specs=[
                pl.BlockSpec((senders, 1, slots, rows, BLOCK), lambda p, g, pr, ct: (0, p, 0, 0, 0)),
            ],
            out_specs=pl.BlockSpec((1, group, BLOCK, BLOCK), lambda p, g, pr, ct: (p, g, 0, 0)),
        ),
        compiler_params=pltpu.CompilerParams(vmem_limit_bytes=48 << 20),
    )(pairs.reshape(parts, tiles * 2), counts, columns)


def body(parts, per_part, jacobian, obs_weight, block_order, tile_pairs, tile_count):
    root_weight = jnp.sqrt(obs_weight)[:, None]
    outgoing = order_columns(jacobian, root_weight, block_order, parts, per_part)
    arrived = lax.all_to_all(outgoing, "obs", split_axis=0, concat_axis=0, tiled=True)
    live = jnp.broadcast_to(tile_count[:, None, None], (1, 1, 2))
    listed = jnp.concatenate([tile_pairs, live], axis=1)
    if parts > 1:
        listed = lax.all_gather(listed, "part", axis=0, tiled=True)
    tiles = partial_tiles(arrived, listed[:, :-1], listed[:, -1, 0])
    tiles = tiles.reshape(-1, BLOCK, BLOCK)
    axes = ("part", "tile") if parts > 1 else "tile"
    return lax.psum_scatter(tiles, axes, scatter_dimension=0, tiled=True)


def solution(mesh):
    owners, tile_size = mesh.devices.shape
    parts = PARTS if owners % PARTS == 0 else 1
    per_part = owners // parts
    devices = mesh.devices.reshape(parts, per_part, tile_size)
    split_mesh = Mesh(devices, ("part", "obs", "tile"))
    every = ("part", "obs", "tile")
    return jax.shard_map(
        functools.partial(body, parts, per_part),
        mesh=split_mesh,
        in_specs=(P(every, None), P(every), P(), P(("part", "obs"), None, None), P(("part", "obs"))),
        out_specs=P(every, None, None),
        check_vma=False,
    )
```

time: 875 us -> 255 us (0.29)
  local copies, waits for them, and re-layouts: 418 us -> 1.89 us
  matrix products: 143 us -> 0 us
  waiting for transfers between devices: 227 us -> 117 us
  blocking collectives: 0 us -> 89.2 us
  other arithmetic: 63.6 us -> 0 us
  Pallas kernels: 0 us -> 25.7 us
    reshape x9 -> x1, local copies, waits for them, and re-layouts: 181 us -> 0.14 us  [partial_tiles(): pairs.reshape(parts, tiles * 2)]
    all_to_all x1, waiting for transfers between devices: 182 us -> 1.64 us  [body(): lax.all_to_all(outgoing, 'obs', split_axis=0, concat_axis=0, tiled=True)]
    dot_general x8 -> x0, matrix products: 143 us -> none  [gram_group(): lax.dot_general(left_cols, columns, (((0,), (0,)), ((), ())), preferred_e...]
    while x8 -> x0, local copies, waits for them, and re-layouts: 138 us -> none
    all_gather x0 -> x1, blocking collectives: none -> 89.2 us  [body(): listed = lax.all_gather(listed, 'part', axis=0, tiled=True)]
    gather x11 -> x0, local copies, waits for them, and re-layouts: 88 us -> none  [the longest x3 48.4 us: body(): ordered = jnp.take(blocks, block_order, axis=1)]
    reduce_scatter x1, waiting for transfers between devices: 44.4 us -> 116 us  [body(): return lax.psum_scatter(tiles, axes, scatter_dimension=0, tiled=True)]
    select_n x9 -> x0, other arithmetic: 47.4 us -> none  [the longest x8 46.7 us: gram_group(): return jnp.where(inside[:, None, None], picked, tiles)]
where the time goes in v1:
time: 255 us; the launch traced here: 254 us
  waiting for transfers between devices  117 us (46%)
  blocking collectives  89.2 us (35%)
  Pallas kernels  25.7 us (10%)
  between operations  14.1 us (6%)
  starting transfers between devices  5.76 us (2%)
    reduce_scatter x1, waiting for transfers between devices, body(): return lax.psum_scatter(tiles, axes, scatter_dimension=0, tiled=True)  116 us
    all_gather x1, blocking collectives, body(): listed = lax.all_gather(listed, 'part', axis=0, tiled=True)  89.2 us
    pallas_call x1, Pallas kernels, partial_tiles(): pl.pallas_call(functools.partial(tile_kernel, group), out_shape=jax.Shape...  15.2 us
    pallas_call x1, Pallas kernels, order_columns(): pl.pallas_call(functools.partial(order_kernel, slots, parts, per_part), o...  10.5 us
    all_to_all x1, starting transfers between devices, body(): lax.all_to_all(outgoing, 'obs', split_axis=0, concat_axis=0, tiled=True)  5.72 us
  transfers between devices with their start and end apart: 2, of which 2 were waited for; matrix products, arithmetic and copies ran while one was open for 0% of the time, Pallas kernels for 0%

profile of v1, /device:TPU:3, one launch (start us, length us, event | category | flops | bytes accessed | tf_op | source)
XLA Modules:
  0.0 253.9 jit_solution(353094476082243804)
XLA Ops:
  6.5 0.7 sqrt_bitcast_fusion
  7.2 0.1 copy.11.weight_ref
  7.3 0.0 copy-start
  7.3 0.7 copy-done
  8.0 10.5 %shard_map.55 = bf16[4,2,64,64,128]{4,3,2,1,0:T(8,128)(2,1)} custom-call(s32[512]{0:T(512)S(1)} %copy-done, bf16[64,65536]{1,0:T(8,128)(2,1)} %jac_ref.1, f32[64,1]{1,0:T(8,128)S(1)} %copy.11.weight_ref), custom_call_target="tpu_custom_call" | custom-call | tf_op jit(solution)/shard_map/pallas_call | solution.py:30
  18.4 0.0 copy-start.1
  18.4 5.7 %all-to-all-start = ((bf16[4,2,64,64,128]{4,3,2,1,0:T(8,128)(2,1)}), bf16[4,2,64,64,128]{4,3,2,1,0:T(8,128)(2,1)}, u32[]{:S(2)}, u32[]{:S(2)}) async-start(bf16[4,2,64,64,128]{4,3,2,1,0:T(8,128)(2,1)} %shard_map.55), calls=%async_computation | async-start | bytes 16777216 | tf_op jit(solution)/shard_map/all_to_all | solution.py:94
  24.2 0.0 reduce-scatter.2.cloned.1.call-start
  24.9 0.0 copy-done.1
  24.9 89.2 %all_gather.3 = s32[2,65,2]{1,2,0:T(2,128)S(1)} all-gather(s32[1,65,2]{1,2,0:T(2,128)S(1)} %concatenate.3), channel_id=1, replica_groups=mesh['part'=2,'obs'=4,'tile'=4] {'part'}, dimensions={0}, use_global_device_ids=true | all-gather | bytes 1560 | tf_op jit(solution)/shard_map/all_gather | solution.py:98
  114.1 0.1 copy.10
  114.2 0.1 reshape.9.pairs_ref
  114.3 0.2 slice_reduce_fusion.count_ref
  114.5 1.6 all-to-all-done.cols_ref
  116.2 15.2 %shard_map.56 = f32[2,64,128,128]{3,2,1,0:T(8,128)} custom-call(s32[2,128]{1,0:T(2,128)S(1)} %reshape.9.pairs_ref, s32[2]{0:T(128)S(1)} %slice_reduce_fusion.count_ref, bf16[4,2,64,64,128]{4,3,2,1,0:T(8,128)(2,1)} %all-to-all-done.cols_ref), custom_call_target="tpu_custom_call" | custom-call | tf_op jit(solution)/shard_map/pallas_call | solution.py:76
  131.4 0.0 reduce-scatter.2.cloned.1.call-update
  131.4 115.7 %reduce-scatter.2.cloned.1.call-done = f32[16,128,128]{2,1,0:T(8,128)} async-done(((f32[128,128,128]{2,1,0:T(8,128)}), f32[16,128,128]{2,1,0:T(8,128)}) %reduce-scatter.2.cloned.1.call-update) | async-done | bytes 1048592 | tf_op jit(solution)/shard_map/reduce_scatter | solution.py:102
  (1 shorter events, 0.0 us)
Async XLA Ops:
  7.3 0.7 copy-start
  18.4 6.4 %copy-start.1 = (s32[1,64,2]{1,2,0:T(2,128)S(1)}, s32[1,64,2]{1,2,0:T(2,128)}, u32[]{:S(2)}) copy-start(s32[1,64,2]{1,2,0:T(2,128)} %param.8) | copy-start | bytes 1540
  18.4 97.7 %all-to-all-start = ((bf16[4,2,64,64,128]{4,3,2,1,0:T(8,128)(2,1)}), bf16[4,2,64,64,128]{4,3,2,1,0:T(8,128)(2,1)}, u32[]{:S(2)}, u32[]{:S(2)}) async-start(bf16[4,2,64,64,128]{4,3,2,1,0:T(8,128)(2,1)} %shard_map.55), calls=%async_computation | async-start | bytes 16777216 | tf_op jit(solution)/shard_map/all_to_all | solution.py:94
  24.2 222.9 %reduce-scatter.2.cloned.1.call-start = ((), (), s32[]{:S(2)}) async-start(), calls=%async_computation.2 | async-start | bytes 9437184 | tf_op jit(solution)/shard_map/reduce_scatter | solution.py:102
Sparse Core Ops, SparseCore 0:
  131.5 115.5 reduce-scatter.1

commit v2 on v1

--- a/solution.py
+++ b/solution.py
@@ -88,23 +88,38 @@
     )(pairs.reshape(parts, tiles * 2), counts, columns)
 
 
+def part_tiles(columns, listed):
+    tiles = partial_tiles(columns, listed[:, :-1], listed[:, -1, 0])
+    return tiles.reshape(-1, BLOCK, BLOCK)
+
+
 def body(parts, per_part, jacobian, obs_weight, block_order, tile_pairs, tile_count):
     root_weight = jnp.sqrt(obs_weight)[:, None]
-    outgoing = order_columns(jacobian, root_weight, block_order, parts, per_part)
-    arrived = lax.all_to_all(outgoing, "obs", split_axis=0, concat_axis=0, tiled=True)
     live = jnp.broadcast_to(tile_count[:, None, None], (1, 1, 2))
     listed = jnp.concatenate([tile_pairs, live], axis=1)
-    if parts > 1:
-        listed = lax.all_gather(listed, "part", axis=0, tiled=True)
-    tiles = partial_tiles(arrived, listed[:, :-1], listed[:, -1, 0])
-    tiles = tiles.reshape(-1, BLOCK, BLOCK)
-    axes = ("part", "tile") if parts > 1 else "tile"
-    return lax.psum_scatter(tiles, axes, scatter_dimension=0, tiled=True)
+    swap = [(0, 1), (1, 0)]
+    here = lax.axis_index("part")
+    orders = block_order.reshape(parts, -1)
+    own_order = lax.dynamic_index_in_dim(orders, here, 0, keepdims=False)
+    far_order = lax.dynamic_index_in_dim(orders, 1 - here, 0, keepdims=False)
+
+    far_listed = lax.ppermute(listed, "part", swap)
+    far_out = order_columns(jacobian, root_weight, far_order, 1, per_part)
+    far_out, far_listed = lax.optimization_barrier((far_out, far_listed))
+    far_columns = lax.all_to_all(far_out, "obs", split_axis=0, concat_axis=0, tiled=True)
+    own_out = order_columns(jacobian, root_weight, own_order, 1, per_part)
+    far_columns, own_out = lax.optimization_barrier((far_columns, own_out))
+    own_columns = lax.all_to_all(own_out, "obs", split_axis=0, concat_axis=0, tiled=True)
+
+    far_sum = lax.psum_scatter(part_tiles(far_columns, far_listed), "tile", scatter_dimension=0, tiled=True)
+    from_far = lax.ppermute(far_sum, "part", swap)
+    own_sum = lax.psum_scatter(part_tiles(own_columns, listed), "tile", scatter_dimension=0, tiled=True)
+    return own_sum + from_far
 
 
 def solution(mesh):
     owners, tile_size = mesh.devices.shape
-    parts = PARTS if owners % PARTS == 0 else 1
+    parts = PARTS
     per_part = owners // parts
     devices = mesh.devices.reshape(parts, per_part, tile_size)
     split_mesh = Mesh(devices, ("part", "obs", "tile"))

time: 255 us -> 209 us (0.82); the launches traced: 254 us -> 205 us
  blocking collectives: 89.2 us -> 0 us
  waiting for transfers between devices: 117 us -> 131 us
  starting transfers between devices: 5.76 us -> 19.6 us
  local copies, waits for them, and re-layouts: 1.89 us -> 11 us
    reduce_scatter x1 -> x2, waiting for transfers between devices: 116 us -> 0.45 us  [the longest x1 0.43 us: body(): lax.psum_scatter(part_tiles(own_columns, listed), 'tile', scatter_dimensi...]
    all_gather x1 -> x0, blocking collectives: 89.2 us -> none  [body(): listed = lax.all_gather(listed, 'part', axis=0, tiled=True)]
    all_to_all x1 -> x2, waiting for transfers between devices: 1.64 us -> 83.8 us  [the longest x1 46.3 us: body(): lax.all_to_all(own_out, 'obs', split_axis=0, concat_axis=0, tiled=True)]
    ppermute x0 -> x2, waiting for transfers between devices: none -> 46.6 us  [the longest x1 46.6 us: body(): from_far = lax.ppermute(far_sum, 'part', swap)]
    all_to_all x1 -> x2, starting transfers between devices: 5.72 us -> 17.2 us  [the longest x1 12.2 us: body(): lax.all_to_all(own_out, 'obs', split_axis=0, concat_axis=0, tiled=True)]
    unnamed x4 -> x11, local copies, waits for them, and re-layouts: 0.69 us -> 7.89 us
    pallas_call x1 -> x2, Pallas kernels: 10.5 us -> 11.9 us  [order_columns(): pl.pallas_call(functools.partial(order_kernel, slots, parts, per_part), o...]
    pallas_call x1 -> x2, Pallas kernels: 15.2 us -> 15.3 us  [partial_tiles(): pl.pallas_call(functools.partial(tile_kernel, group), out_shape=jax.Shape...]
  transfers between devices with their start and end apart: 2 -> 6, of which waited for: 2 -> 4; matrix products, arithmetic and copies ran while one was open for 0% -> 1% of each run, Pallas kernels for 0% -> 9%
where the time goes in v2:
time: 209 us; the launch traced here: 205 us
  waiting for transfers between devices  131 us (63%)
  Pallas kernels  27.2 us (13%)
  starting transfers between devices  19.6 us (9%)
  between operations  14.2 us (7%)
  local copies, waits for them, and re-layouts  11 us (5%)
  other arithmetic  2.31 us (1%)
    ppermute x1, waiting for transfers between devices, body(): from_far = lax.ppermute(far_sum, 'part', swap)  46.6 us
    all_to_all x1, waiting for transfers between devices, body(): lax.all_to_all(own_out, 'obs', split_axis=0, concat_axis=0, tiled=True)  46.3 us
    all_to_all x1, waiting for transfers between devices, body(): lax.all_to_all(far_out, 'obs', split_axis=0, concat_axis=0, tiled=True)  37.6 us
    pallas_call x2, Pallas kernels, partial_tiles(): pl.pallas_call(functools.partial(tile_kernel, group), out_shape=jax.Shape...  15.3 us
    all_to_all x1, starting transfers between devices, body(): lax.all_to_all(own_out, 'obs', split_axis=0, concat_axis=0, tiled=True)  12.2 us
    pallas_call x2, Pallas kernels, order_columns(): pl.pallas_call(functools.partial(order_kernel, slots, parts, per_part), o...  11.9 us
    unnamed x11, local copies, waits for them, and re-layouts  7.89 us
    all_to_all x1, starting transfers between devices, body(): lax.all_to_all(far_out, 'obs', split_axis=0, concat_axis=0, tiled=True)  5.04 us
  transfers between devices with their start and end apart: 6, of which 4 were waited for; matrix products, arithmetic and copies ran while one was open for 1% of the time, Pallas kernels for 9%

profile of v2, /device:TPU:3, one launch (start us, length us, event | category | flops | bytes accessed | tf_op | source)
XLA Modules:
  0.0 205.1 jit_solution(1034513720181340515)
XLA Ops:
  7.2 0.7 concatenate.3
  7.9 2.3 %collective-permute-start = (s32[1,65,2]{1,2,0:T(2,128)S(1)}, s32[1,65,2]{1,2,0:T(2,128)S(1)}, u32[]{:S(2)}, u32[]{:S(2)}) collective-permute-start(s32[1,65,2]{1,2,0:T(2,128)S(1)} %concatenate.3), channel_id=1, source_target_pairs={{0,16},{16,0},{1,17},{17,1},{2,18},{18,2},{3,19},{19,3},{4,20},{20... | collective-permute-start | bytes 1568 | tf_op jit(solution)/shard_map/ppermute | solution.py:106
  10.2 0.7 reshape.21
  10.9 0.7 sqrt_bitcast_fusion
  11.5 0.1 copy.11.weight_ref
  11.6 5.9 %shard_map.55 = bf16[4,1,64,64,128]{4,3,2,1,0:T(8,128)(2,1)S(1)} custom-call(s32[256]{0:T(256)S(1)} %bitcast.13, bf16[64,65536]{1,0:T(8,128)(2,1)} %jac_ref.3, f32[64,1]{1,0:T(8,128)S(1)} %copy.11.weight_ref), custom_call_target="tpu_custom_call" | custom-call | tf_op jit(solution)/shard_map/pallas_call | solution.py:30
  17.6 0.0 copy-start.1
  17.6 1.9 copy-done.1
  19.6 0.0 collective-permute-done
  19.6 5.0 %all-to-all-start = ((bf16[4,1,64,64,128]{4,3,2,1,0:T(8,128)(2,1)}), bf16[4,1,64,64,128]{4,3,2,1,0:T(8,128)(2,1)}, u32[]{:S(2)}, u32[]{:S(2)}) async-start(bf16[4,1,64,64,128]{4,3,2,1,0:T(8,128)(2,1)} %copy-done.1), calls=%async_computation | async-start | bytes 8388608 | tf_op jit(solution)/shard_map/all_to_all | solution.py:109
  24.6 0.0 reduce-scatter.5.cloned.1.call-start
  24.6 5.9 %shard_map.56 = bf16[4,1,64,64,128]{4,3,2,1,0:T(8,128)(2,1)S(1)} custom-call(s32[256]{0:T(256)S(1)} %bitcast.12, bf16[64,65536]{1,0:T(8,128)(2,1)} %jac_ref.3, f32[64,1]{1,0:T(8,128)S(1)} %copy.11.weight_ref), custom_call_target="tpu_custom_call" | custom-call | tf_op jit(solution)/shard_map/pallas_call | solution.py:30
  30.6 0.0 copy-start
  30.6 1.9 copy-done
  32.5 0.6 slice.8
  33.1 0.1 copy.13
  33.2 0.1 reshape.23.pairs_ref
  33.4 37.6 %all-to-all-done.cols_ref = bf16[4,1,64,64,128]{4,3,2,1,0:T(8,128)(2,1)} async-done(((bf16[4,1,64,64,128]{4,3,2,1,0:T(8,128)(2,1)}), bf16[4,1,64,64,128]{4,3,2,1,0:T(8,128)(2,1)}, u32[]{:S(2)}, u32[]{:S(2)}) %all-to-all-start) | async-done | bytes 4194336 | tf_op jit(solution)/shard_map/all_to_all | solution.py:109
  70.9 8.6 %shard_map.58 = f32[1,64,128,128]{3,2,1,0:T(8,128)S(1)} custom-call(s32[1,128]{1,0:T(1,128)S(1)} %reshape.23.pairs_ref, s32[1]{0:T(128)} %bitcast.5.count_ref, bf16[4,1,64,64,128]{4,3,2,1,0:T(8,128)(2,1)} %all-to-all-done.cols_ref), custom_call_target="tpu_custom_call" | custom-call | tf_op jit(solution)/shard_map/pallas_call | solution.py:76
  79.5 0.0 copy-start.2
  79.5 2.0 copy-done.2
  81.5 0.0 reduce-scatter.5.cloned.1.call-update
  81.5 0.0 copy-start.4
  81.5 12.2 %all-to-all-start.1 = ((bf16[4,1,64,64,128]{4,3,2,1,0:T(8,128)(2,1)}), bf16[4,1,64,64,128]{4,3,2,1,0:T(8,128)(2,1)}, u32[]{:S(2)}, u32[]{:S(2)}) async-start(bf16[4,1,64,64,128]{4,3,2,1,0:T(8,128)(2,1)} %copy-done), calls=%async_computation.1 | async-start | bytes 8388608 | tf_op jit(solution)/shard_map/all_to_all | solution.py:112
  93.7 0.0 reduce-scatter.3.cloned.1.call-start
  93.7 0.0 copy-done.4
  93.7 0.1 copy.10
  93.8 0.1 reshape.20.pairs_ref
  93.9 46.3 %all-to-all-done.1.cols_ref = bf16[4,1,64,64,128]{4,3,2,1,0:T(8,128)(2,1)} async-done(((bf16[4,1,64,64,128]{4,3,2,1,0:T(8,128)(2,1)}), bf16[4,1,64,64,128]{4,3,2,1,0:T(8,128)(2,1)}, u32[]{:S(2)}, u32[]{:S(2)}) %all-to-all-start.1) | async-done | bytes 4194336 | tf_op jit(solution)/shard_map/all_to_all | solution.py:112
  140.2 6.7 %shard_map.57 = f32[1,64,128,128]{3,2,1,0:T(8,128)S(1)} custom-call(s32[1,128]{1,0:T(1,128)S(1)} %reshape.20.pairs_ref, s32[1]{0:T(128)} %copy.14.count_ref, bf16[4,1,64,64,128]{4,3,2,1,0:T(8,128)(2,1)} %all-to-all-done.1.cols_ref), custom_call_target="tpu_custom_call" | custom-call | tf_op jit(solution)/shard_map/pallas_call | solution.py:76
  146.9 0.0 copy-start.3
  146.9 1.9 copy-done.3
  148.8 0.0 reduce-scatter.3.cloned.1.call-update
  148.9 0.0 reduce-scatter.5.cloned.1.call-done
  148.9 0.1 collective-permute-start.1
  149.0 46.6 %collective-permute-done.1 = f32[16,128,128]{2,1,0:T(8,128)S(1)} collective-permute-done((f32[16,128,128]{2,1,0:T(8,128)}, f32[16,128,128]{2,1,0:T(8,128)S(1)}, u32[]{:S(2)}, u32[]{:S(2)}) %collective-permute-start.1) | collective-permute-done | bytes 1048608 | tf_op jit(solution)/shard_map/ppermute | solution.py:115
  195.6 0.4 reduce-scatter.3.cloned.1.call-done
  196.0 2.3 %add.19 = f32[16,128,128]{2,1,0:T(8,128)} add(f32[16,128,128]{2,1,0:T(8,128)} %reduce-scatter.3.cloned.1.call-done, f32[16,128,128]{2,1,0:T(8,128)S(1)} %collective-permute-done.1) | non-fusion elementwise | flops 262144 | bytes 3145728 | tf_op jit(solution)/shard_map/add | solution.py:117
  (1 shorter events, 0.0 us)
Async XLA Ops:
  7.9 11.7 %collective-permute-start = (s32[1,65,2]{1,2,0:T(2,128)S(1)}, s32[1,65,2]{1,2,0:T(2,128)S(1)}, u32[]{:S(2)}, u32[]{:S(2)}) collective-permute-start(s32[1,65,2]{1,2,0:T(2,128)S(1)} %concatenate.3), channel_id=1, source_target_pairs={{0,16},{16,0},{1,17},{17,1},{2,18},{18,2},{3,19},{19,3},{4,20},{20... | collective-permute-start | bytes 1568 | tf_op jit(solution)/shard_map/ppermute | solution.py:106
  17.6 2.0 copy-start.1
  19.6 51.3 %all-to-all-start = ((bf16[4,1,64,64,128]{4,3,2,1,0:T(8,128)(2,1)}), bf16[4,1,64,64,128]{4,3,2,1,0:T(8,128)(2,1)}, u32[]{:S(2)}, u32[]{:S(2)}) async-start(bf16[4,1,64,64,128]{4,3,2,1,0:T(8,128)(2,1)} %copy-done.1), calls=%async_computation | async-start | bytes 8388608 | tf_op jit(solution)/shard_map/all_to_all | solution.py:109
  24.6 124.3 %reduce-scatter.5.cloned.1.call-start = ((), (), s32[]{:S(2)}) async-start(), calls=%async_computation.5 | async-start | bytes 5242880 | tf_op jit(solution)/shard_map/reduce_scatter | solution.py:114
  30.6 2.0 copy-start
  79.5 2.0 copy-start.2
  81.5 12.2 %copy-start.4 = (s32[1,64,2]{1,2,0:T(2,128)S(1)}, s32[1,64,2]{1,2,0:T(2,128)}, u32[]{:S(2)}) copy-start(s32[1,64,2]{1,2,0:T(2,128)} %param.8) | copy-start | bytes 1540
  81.5 58.7 %all-to-all-start.1 = ((bf16[4,1,64,64,128]{4,3,2,1,0:T(8,128)(2,1)}), bf16[4,1,64,64,128]{4,3,2,1,0:T(8,128)(2,1)}, u32[]{:S(2)}, u32[]{:S(2)}) async-start(bf16[4,1,64,64,128]{4,3,2,1,0:T(8,128)(2,1)} %copy-done), calls=%async_computation.1 | async-start | bytes 8388608 | tf_op jit(solution)/shard_map/all_to_all | solution.py:112
  93.7 102.3 %reduce-scatter.3.cloned.1.call-start = ((), (), s32[]{:S(2)}) async-start(), calls=%async_computation.4 | async-start | bytes 5242880 | tf_op jit(solution)/shard_map/reduce_scatter | solution.py:116
  146.9 2.0 copy-start.3
  148.9 46.7 %collective-permute-start.1 = (f32[16,128,128]{2,1,0:T(8,128)}, f32[16,128,128]{2,1,0:T(8,128)S(1)}, u32[]{:S(2)}, u32[]{:S(2)}) collective-permute-start(f32[16,128,128]{2,1,0:T(8,128)} %reduce-scatter.5.cloned.1.call-done), channel_id=1, source_target_pairs={{0,16},{16,0},{1,17},{17,1},{2,18},{18,2},{3,19},{19,3},{4,20},{20... | collective-permute-start | bytes 3145736 | tf_op jit(solution)/shard_map/ppermute | solution.py:115
Sparse Core Ops, SparseCore 0:
  81.6 51.9 reduce-scatter.4
  149.0 46.9 reduce-scatter.2
